TPU v7x, 256 devices: a whole 4x4x8 slice. The times are simulated.
256 devices in a mesh: pat: 32 (over x, y, z_hi), code: 8 (over z_lo, core).
Axes of the slice: x: 4, y: 4, z: 8 (z_hi: 2, z_lo: 4; z = z_hi * 4 + z_lo), core: 2. Of those that a mesh axis runs over, the one named last changes fastest.
Arguments:
- tiles: bfloat16 [768, 128, 120, 128], P(('pat', 'code')), may hold values from 0 to 32
- patient_block: int32 [768], P(('pat', 'code')), may hold values from 0 to 3
- owner: int32 [768, 1], P(('pat', 'code')), may hold values from 0 to 31
- sub_block: int32 [768], P(('pat', 'code')), may hold values from 0 to 1
- live: int32 [768], P(('pat', 'code')), may hold values 0 or 1
- code_factor: bfloat16 [65536, 256], P(('pat', 'code')), may hold values from -0.00390625 to 0.01171875
- month_factor: float32 [120, 256], replicated, may hold values from -0.0913 to 0.2739
Outputs:
- patient_factor: float32 [16384, 256], P(('pat', 'code'))
All inputs are finite; a program needn't handle non-finite values. No bound on the sum of `live` on one device may be relied on, other than what follows from the above.
Results may differ from a plain program's by a relative error of at most 0.0003.
Values may be sent and summed in bfloat16 or wider, within the bound.
A program may use at most 128 MiB of HBM per device.

v0:
```python
import jax
import jax.numpy as jnp
from jax import lax
from jax.sharding import PartitionSpec as P

PATB = 4


def local(tiles, patient_block, owner, sub_block, live, code_factor, month_factor):
    slots = tiles.shape[0]
    block = tiles.shape[1]
    months = tiles.shape[2]
    rank = code_factor.shape[1]
    own = code_factor.shape[0] // block
    month_gram = jnp.dot(
        month_factor.T,
        month_factor,
        precision=lax.Precision.HIGHEST,
        preferred_element_type=jnp.float32,
    )
    gathered = lax.all_gather(code_factor, "pat", axis=0, tiled=True)
    local_gram = jnp.dot(code_factor.T, code_factor, preferred_element_type=jnp.float32)
    code_gram = lax.psum(local_gram, ("pat", "code"))
    partial_rows = jnp.zeros((PATB * block, rank), jnp.float32)
    for index in range(slots):
        start = (owner[index, 0] * own + sub_block[index]) * block
        code_block = lax.dynamic_slice_in_dim(gathered, start, block, 0)
        counts_tile = tiles[index]

        def contract(unused, counts_tile=counts_tile, code_block=code_block):
            wide = jnp.dot(
                counts_tile.reshape(block * months, block),
                code_block,
                preferred_element_type=jnp.float32,
            )
            return jnp.sum(wide.reshape(block, months, rank) * month_factor[None], axis=1)

        def nothing(unused):
            return jnp.zeros((block, rank), jnp.float32)

        piece = lax.cond(live[index] > 0, contract, nothing, 0)
        start = patient_block[index] * block
        current = lax.dynamic_slice_in_dim(partial_rows, start, block, 0)
        partial_rows = lax.dynamic_update_slice_in_dim(partial_rows, current + piece, start, 0)
    gram = code_gram * month_gram
    lower = jnp.linalg.cholesky(gram)
    shares = lax.psum_scatter(partial_rows, "code", scatter_dimension=0, tiled=True)
    return jax.scipy.linalg.cho_solve((lower, True), shares.T).T


def solution(mesh):
    placed = (
        P(("pat", "code"), None, None, None),
        P(("pat", "code")),
        P(("pat", "code"), None),
        P(("pat", "code")),
        P(("pat", "code")),
        P(("pat", "code"), None),
        P(),
    )
    return jax.shard_map(
        local, mesh=mesh, in_specs=placed, out_specs=P(("pat", "code"), None), check_vma=False
    )
```

profile of v0, /device:TPU:1, one launch (start us, length us, event | category | flops | bytes accessed | tf_op | source)
XLA Modules:
  0.0 435.2 jit_solution(1730634419115906238)
XLA Ops:
  7.4 1.9 fusion.26
  9.4 1.7 copy.25
  11.1 1.4 fusion.25
  14.6 1.4 fusion.24
  18.1 285.5 %all-reduce.3.cloned.1.call-done = f32[256,256]{0,1:T(8,128)} async-done(((f32[256,256]{0,1:T(8,128)}), f32[256,256]{0,1:T(8,128)}) %all-reduce.3.cloned.1.call-update) | async-done | bytes 262160 | tf_op jit(solution)/shard_map/psum | solution.py:23
  303.6 1.5 convolution_multiply_fusion
  305.3 11.7 %cholesky.50 = f32[128,128]{1,0:T(8,128)S(1)} custom-call(f32[128,128]{1,0:T(8,128)S(1)} %cholesky.118), custom_call_target="Cholesky" | custom-call | tf_op jit(solution)/shard_map/jit(cholesky)/cholesky | solution.py:46
  317.0 9.8 %custom-call.18 = f32[1,128,128]{1,2,0:T(8,128)S(1)} custom-call(f32[1,128,128]{2,1,0:T(8,128)S(1)} %get-tuple-element.245), custom_call_target="InvertDiagBlocksLowerTriangular" | custom-call | tf_op jit(solution)/shard_map/jit(cholesky)/cholesky | solution.py:46
  327.4 11.7 %cholesky.105 = f32[128,128]{1,0:T(8,128)S(1)} custom-call(f32[128,128]{1,0:T(8,128)S(1)} %convolution_subtract_fusion), custom_call_target="Cholesky" | custom-call | tf_op jit(solution)/shard_map/jit(cholesky)/cholesky | solution.py:46
  339.1 17.7 %conditional.5 = (f32[128,256]{0,1:T(8,128)S(1)}) conditional(s32[]{:T(128)} %bitcast.24, () %tuple.33, (s32[3,1]{0,1:T(1,128)}, bf16[8192,256]{0,1:T(8,128)(2,1)}, bf16[3,128,120,128]{3,2,1,0:T(8,128)(2,1)}, f32[120,256]{1,0:T(8,128)}, s32[]{:T(128)}, /*index=5*/s32[3]{0:T(128)}, s32[1,1]{0,1:T(1,128)}) %tuple.38), branch_computations={%region_11.12_spmd, %region_12.14_spmd} | conditional | flops 1014464512 | bytes 28336252 | solution.py:41
  339.3 1.3 slice.130
  343.1 7.1 %copy.28 = bf16[3,128,120,128]{3,1,2,0:T(8,128)(2,1)S(1)} copy(bf16[3,128,120,128]{3,2,1,0:T(8,128)(2,1)} %get-tuple-element.227) | data formatting | bytes 23592960 | tf_op jit(solution)/shard_map
  350.2 6.6 %fusion.8 = f32[128,256]{0,1:T(8,128)S(1)} fusion(f32[120,256]{1,0:T(8,128)S(1)} %copy-done, bf16[3,128,120,128]{3,1,2,0:T(8,128)(2,1)S(1)} %copy.28, bf16[8192,256]{0,1:T(8,128)(2,1)} %get-tuple-element.127, s32[]{:T(128)S(6)} %select_n.25), kind=kOutput, calls=%fused_computation.13 | convolution fusion | flops 1014464512 | bytes 4251652 | tf_op jit(solution)/shard_map/cond/branch_1_fun/dot_general | solution.py:31
  356.8 17.6 %conditional.4 = (f32[128,256]{0,1:T(8,128)S(1)}) conditional(s32[]{:T(128)} %bitcast.22, () %tuple.31, (s32[3,1]{0,1:T(1,128)}, bf16[8192,256]{0,1:T(8,128)(2,1)}, bf16[3,128,120,128]{3,2,1,0:T(8,128)(2,1)}, f32[120,256]{1,0:T(8,128)}, s32[]{:T(128)}, /*index=5*/s32[3]{0:T(128)}, s32[1,1]{0,1:T(1,128)}) %tuple.38), branch_computations={%region_8.9_spmd, %region_9.11_spmd} | conditional | flops 1014464512 | bytes 28336252 | solution.py:41
  360.6 7.1 %copy.27 = bf16[3,128,120,128]{3,1,2,0:T(8,128)(2,1)S(1)} copy(bf16[3,128,120,128]{3,2,1,0:T(8,128)(2,1)} %get-tuple-element.220) | data formatting | bytes 23592960 | tf_op jit(solution)/shard_map
  367.8 6.6 %fusion.4 = f32[128,256]{0,1:T(8,128)S(1)} fusion(f32[120,256]{1,0:T(8,128)S(1)} %copy-done.1, bf16[3,128,120,128]{3,1,2,0:T(8,128)(2,1)S(1)} %copy.27, bf16[8192,256]{0,1:T(8,128)(2,1)} %get-tuple-element.123, s32[]{:T(128)S(6)} %select_n.24), kind=kOutput, calls=%fused_computation.7 | convolution fusion | flops 1014464512 | bytes 4251652 | tf_op jit(solution)/shard_map/cond/branch_1_fun/dot_general | solution.py:31
  374.4 15.1 %conditional.3 = (f32[128,256]{0,1:T(8,128)S(1)}) conditional(s32[]{:T(128)} %bitcast.19, () %tuple.29, (s32[3,1]{0,1:T(1,128)}, bf16[8192,256]{0,1:T(8,128)(2,1)}, bf16[3,128,120,128]{3,2,1,0:T(8,128)(2,1)}, f32[120,256]{1,0:T(8,128)}, s32[]{:T(128)}, /*index=5*/s32[3]{0:T(128)}, s32[1,1]{0,1:T(1,128)}) %tuple.38), branch_computations={%region_5.6_spmd, %region_6.8_spmd} | conditional | flops 1014464512 | bytes 28336236 | solution.py:41
  375.7 7.1 %copy.26 = bf16[3,128,120,128]{3,1,2,0:T(8,128)(2,1)S(1)} copy(bf16[3,128,120,128]{3,2,1,0:T(8,128)(2,1)} %get-tuple-element.213) | data formatting | bytes 23592960 | tf_op jit(solution)/shard_map
  382.9 6.6 %fusion = f32[128,256]{0,1:T(8,128)S(1)} fusion(f32[120,256]{1,0:T(8,128)S(1)} %copy-done.2, bf16[3,128,120,128]{3,1,2,0:T(8,128)(2,1)S(1)} %copy.26, bf16[8192,256]{0,1:T(8,128)(2,1)} %get-tuple-element.119, s32[]{:T(128)S(6)} %select_n.23), kind=kOutput, calls=%fused_computation.1 | convolution fusion | flops 1014464512 | bytes 4251652 | tf_op jit(solution)/shard_map/cond/branch_1_fun/dot_general | solution.py:31
  392.8 3.8 while.1
  393.4 1.3 bitcast_dynamic-update-slice_fusion.2
  395.3 1.3 bitcast_dynamic-update-slice_fusion.2
  396.6 19.7 %custom-call.19 = f32[2,128,128]{1,2,0:T(8,128)S(1)} custom-call(f32[2,128,128]{2,1,0:T(8,128)S(1)} %get-tuple-element.168), custom_call_target="InvertDiagBlocksLowerTriangular" | custom-call | tf_op jit(solution)/shard_map/jit(_cho_solve)/triangular_solve | solution.py:48
  416.3 7.9 %reduce-scatter.4.cloned.1.call-done = f32[64,256]{1,0:T(8,128)} async-done(((f32[512,256]{1,0:T(8,128)}), f32[64,256]{1,0:T(8,128)}) %reduce-scatter.4.cloned.1.call-update) | async-done | bytes 65552 | tf_op jit(solution)/shard_map/reduce_scatter | solution.py:47
  (45 shorter events, 11.2 us)
Async XLA Ops:
  7.4 296.2 %all-reduce.3.cloned.1.call-start = ((), (), s32[]{:S(2)}) async-start(), calls=%async_computation.1 | async-start | bytes 524288 | tf_op jit(solution)/shard_map/psum | solution.py:23
  9.3 329.8 %all-gather.2.cloned.1.call-start = ((), (), s32[]{:S(2)}) async-start(), calls=%async_computation.2 | async-start | bytes 4325376 | tf_op jit(solution)/shard_map/all_gather | solution.py:21
  11.0 413.2 %reduce-scatter.4.cloned.1.call-start = ((), (), s32[]{:S(2)}) async-start(), calls=%async_computation.3 | async-start | bytes 589824 | tf_op jit(solution)/shard_map/reduce_scatter | solution.py:47
  343.1 7.2 %copy-start = (f32[120,256]{1,0:T(8,128)S(1)}, f32[120,256]{1,0:T(8,128)}, u32[]{:S(2)}) copy-start(f32[120,256]{1,0:T(8,128)} %get-tuple-element.130) | copy-start | bytes 368644 | tf_op jit(solution)/shard_map/cond
  360.6 7.2 %copy-start.1 = (f32[120,256]{1,0:T(8,128)S(1)}, f32[120,256]{1,0:T(8,128)}, u32[]{:S(2)}) copy-start(f32[120,256]{1,0:T(8,128)} %get-tuple-element.126) | copy-start | bytes 368644 | tf_op jit(solution)/shard_map/cond
  375.7 7.2 %copy-start.2 = (f32[120,256]{1,0:T(8,128)S(1)}, f32[120,256]{1,0:T(8,128)}, u32[]{:S(2)}) copy-start(f32[120,256]{1,0:T(8,128)} %get-tuple-element.122) | copy-start | bytes 368644 | tf_op jit(solution)/shard_map/cond
Sparse Core Ops, SparseCore 0:
  13.6 289.9 all-reduce.2
Sparse Core Ops, SparseCore 1:
  13.0 129.5 all-gather.1
  390.8 33.4 reduce-scatter.3
where the time goes:
time: 438 us; the launch traced here: 435 us
  waiting for transfers between devices  294 us (67%)
  other arithmetic  54.5 us (12%)
  local copies, waits for them, and re-layouts  36.1 us (8%)
  matrix products  26.4 us (6%)
  between operations  20.4 us (5%)
    psum x1, waiting for transfers between devices, local(): code_gram = lax.psum(local_gram, ('pat', 'code'))  285 us
    another operation x6, other arithmetic, local(): lower = jnp.linalg.cholesky(gram)  34 us
    another operation x9, local copies, waits for them, and re-layouts  25.3 us
    dot_general x3, matrix products, contract(): jnp.dot(counts_tile.reshape(block * months, block), code_block, preferred...  19.8 us
    another operation x3, other arithmetic, local(): return jax.scipy.linalg.cho_solve((lower, True), shares.T).T  19.7 us
  transfers between devices with their start and end apart: 3, of which 2 were waited for; matrix products, arithmetic and copies ran while one was open for 15% of the time, Pallas kernels for 0%

commit v1 on v0

v1 whole, which is shorter than its diff:
```python
import jax
import jax.numpy as jnp
from jax import lax
from jax.experimental import pallas as pl
from jax.experimental.pallas import tpu as pltpu
from jax.sharding import PartitionSpec as P

MESH = pl.DeviceIdType.MESH
HI = lax.Precision.HIGHEST
F32 = jnp.float32
BLOCK = 128
MONTHS = 120
RANK = 256
SLOTS = 3
HALF = 64
CHUNK = 32
SIDE = 64


def recip(p):
    r = pltpu.reciprocal(p, approx=True)
    r = r * (2.0 - p * r)
    return r * (2.0 - p * r)


def sweep(x, n):
    rows = lax.broadcasted_iota(jnp.int32, x.shape, 0)
    cols = lax.broadcasted_iota(jnp.int32, x.shape, 1)
    for k in range(n):
        row, col = x[k : k + 1, :], x[:, k : k + 1]
        inv = recip(x[k : k + 1, k : k + 1])
        w = row * inv
        y = x - col * w
        y = jnp.where(cols == k, col * inv, y)
        x = jnp.where(rows == k, jnp.where(cols == k, -inv, w), y)
    return x


def negative_inverse(a):
    for o in range(0, RANK, SIDE):
        small = sweep(a[o : o + SIDE, o : o + SIDE], SIDE)
        rows = a[o : o + SIDE, :]
        w = -jnp.dot(small, rows, precision=HI, preferred_element_type=F32)
        u = lax.dot_general(
            rows, w, (((0,), (0,)), ((), ())), precision=HI, preferred_element_type=F32
        )
        a[...] = a[...] - u
        a[o : o + SIDE, :] = w
        a[:, o : o + SIDE] = w.T
        a[o : o + SIDE, o : o + SIDE] = small


def kernel(
    owner, sub, block_at, live, tiles, code, month, out,
    counts, group, gram_own, plane_in, piece, column_in, whole, gram, month_gram,
    part, pair_in, line_out, line_in,
    tile_sem, zh_s, zh_r, first_s, first_r, second_s, second_r,
    plane_s, plane_r, column_s, column_r, spread_s, spread_r,
    pair_s, pair_r, line_s, line_r,
):
    pat, code_at = lax.axis_index("pat"), lax.axis_index("code")
    x, y, zh = pat // 8, (pat // 2) % 4, pat % 2
    zl, core = code_at // 2, code_at % 2
    z = zh * 4 + zl

    def device(x, y, z, c):
        x, y, z = lax.rem(x, 4), lax.rem(y, 4), lax.rem(z, 8)
        return ((x * 4 + y) * 2 + z // 4, lax.rem(z, 4) * 2 + c)

    def plane(e):
        px, py, pc = lax.rem(x + e // 8, 4), lax.rem(y + (e // 2) % 4, 4), lax.rem(core + e % 2, 2)
        return device(px, py, z, pc), (px * 4 + py) * 2 + pc

    def remote(src, dst, send, recv, to):
        return pltpu.make_async_remote_copy(
            src_ref=src, dst_ref=dst, send_sem=send, recv_sem=recv, device_id=to, device_id_type=MESH
        )

    loads = [
        pltpu.make_async_copy(tiles.at[k], counts.at[k], tile_sem.at[k]) for k in range(SLOTS)
    ]
    for load in loads:
        load.start()

    barrier = pltpu.get_barrier_semaphore()

    def greet(e, _):
        pl.semaphore_signal(barrier, inc=1, device_id=plane(e)[0], device_id_type=MESH)
        return 0

    lax.fori_loop(1, 32, greet, 0)
    for d in range(1, 8):
        pl.semaphore_signal(
            barrier, inc=1, device_id=device(x, y, z + d, core), device_id_type=MESH
        )
    own = lax.dot_general(
        code[...], code[...], (((0,), (0,)), ((), ())), preferred_element_type=F32
    )
    gram_own[...] = own.reshape(32, 8, RANK)
    uv = [(x, y), (y, x)]
    for h in range(2):
        u, v = uv[h]
        group[h, zh, v, u] = code[h * BLOCK : (h + 1) * BLOCK, :]
    pl.semaphore_wait(barrier, 38)

    def first_stage(s, who):
        copies = []
        for h in range(2):
            u, v = uv[h]
            for d in range(1, 4):
                to = device(x + d, y, z, core) if h == 0 else device(x, y + d, z, core)
                here = group.at[h, who, v, u]
                copies.append(
                    remote(here, here, first_s.at[s, h, d - 1], first_r.at[s, h, d - 1], to)
                )
        for c in copies:
            c.start()
        return copies

    def second_stage(s, who):
        copies = []
        for h in range(2):
            u, v = uv[h]
            for d in range(1, 4):
                to = device(x, y + d, z, core) if h == 0 else device(x + d, y, z, core)
                here = group.at[h, who, v]
                copies.append(
                    remote(here, here, second_s.at[s, h, d - 1], second_r.at[s, h, d - 1], to)
                )
        for c in copies:
            c.start()
        return copies

    me = (x * 4 + y) * 2 + core

    def scatter(e, _):
        to, q = plane(e)
        remote(gram_own.at[q], plane_in.at[e - 1], plane_s, plane_r, to).start()
        return 0

    lax.fori_loop(1, 32, scatter, 0)
    first_own = first_stage(0, zh)

    def arrived(buf, sem):
        pltpu.make_async_copy(buf, buf, sem).wait()

    month_gram[...] = lax.dot_general(
        month[...], month[...], (((0,), (0,)), ((), ())), precision=HI, preferred_element_type=F32
    )
    arrived(plane_in, plane_r)
    total = gram_own[me]
    for e in range(31):
        total = total + plane_in[e]
    piece[0] = total
    columns = []
    for d in range(1, 8):
        columns.append(
            remote(
                piece.at[0], column_in.at[d - 1], column_s.at[d - 1], column_r.at[d - 1],
                device(x, y, z + d, core),
            )
        )
    for c in columns:
        c.start()
    across = []
    for h in range(2):
        u, v = uv[h]
        across.append(
            remote(
                code.at[h * BLOCK : (h + 1) * BLOCK, :], group.at[h, zh, v, u],
                zh_s.at[h], zh_r.at[h], device(x, y, z + 4, core),
            )
        )
    for c in across:
        c.start()
    for c in first_own:
        c.wait()
    second_own = second_stage(0, zh)
    for c in columns:
        c.wait()
    total = piece[0]
    for d in range(7):
        total = total + column_in[d]
    piece[1] = total
    whole[me] = total

    def spread(e, _):
        to, _q = plane(e)
        remote(piece.at[1], whole.at[me], spread_s, spread_r, to).start()
        return 0

    lax.fori_loop(1, 32, spread, 0)
    for c in across:
        c.wait()
    first_other = first_stage(1, 1 - zh)
    arrived(whole.at[0:31], spread_r)
    gram[...] = whole[...].reshape(RANK, RANK) * month_gram[...]
    for c in first_other:
        c.wait()
    second_other = second_stage(1, 1 - zh)
    negative_inverse(gram)
    for c in second_own + second_other:
        c.wait()
    for load in loads:
        load.wait()

    blocks = []
    for k in range(SLOTS):
        o, s = owner[k], sub[k]
        ox, oy, oz = o // 8, (o // 2) % 4, o % 2
        ou, ov = jnp.where(s == 0, ox, oy), jnp.where(s == 0, oy, ox)
        blocks.append((s, oz, ov, ou))

    def contract(p):
        pieces = []
        for k in range(SLOTS):
            lhs = counts[k, pl.ds(pl.multiple_of(p * MONTHS, CHUNK * MONTHS), CHUNK * MONTHS), :]
            wide = jnp.dot(lhs, group[blocks[k]], preferred_element_type=F32)
            wide = wide.reshape(CHUNK, MONTHS, RANK) * month[...][None]
            pieces.append(jnp.sum(wide, axis=1) * live[k].astype(F32))
        return pieces

    for which in range(2):
        half = 1 - core if which == 0 else core

        def step(i, _, half=half):
            pieces = contract(half * HALF + i * CHUNK)
            for b in range(4):
                total = jnp.zeros((CHUNK, RANK), F32)
                for k in range(SLOTS):
                    total = total + jnp.where(block_at[k] == b, pieces[k], 0.0)
                part[half, b, pl.ds(pl.multiple_of(i * CHUNK, CHUNK), CHUNK), :] = total
            return 0

        lax.fori_loop(0, HALF // CHUNK, step, 0)
        if which == 0:
            pair = remote(
                part.at[1 - core], pair_in, pair_s, pair_r, device(x, y, z, 1 - core)
            )
            pair.start()
    pair.wait()
    line_out[...] = part[core] + pair_in[...]
    line = []
    for d in range(1, 4):
        zt = lax.rem(zl + d, 4)
        line.append(
            remote(
                line_out.at[zt], line_in.at[d - 1], line_s.at[d - 1], line_r.at[d - 1],
                device(x, y, zh * 4 + zt, core),
            )
        )
    for c in line:
        c.start()
    for c in line:
        c.wait()
    share = line_out[zl] + line_in[0] + line_in[1] + line_in[2]
    out[...] = -jnp.dot(share, gram[...], precision=HI, preferred_element_type=F32)
    arrived(gram_own.at[0:31], plane_s)
    arrived(gram_own.at[0:31], spread_s)


def local(tiles, patient_block, owner, sub_block, live, code_factor, month_factor):
    dma, vmem = pltpu.SemaphoreType.DMA, pltpu.VMEM
    smem_spec = pl.BlockSpec(memory_space=pltpu.SMEM)
    vmem_spec = pl.BlockSpec(memory_space=pltpu.VMEM)
    return pl.pallas_call(
        kernel,
        out_shape=jax.ShapeDtypeStruct((HALF, RANK), F32),
        in_specs=[smem_spec] * 4 + [pl.BlockSpec(memory_space=pl.ANY), vmem_spec, vmem_spec],
        out_specs=vmem_spec,
        scratch_shapes=[
            vmem((SLOTS, BLOCK * MONTHS, BLOCK), jnp.bfloat16),
            vmem((2, 2, 4, 4, BLOCK, RANK), jnp.bfloat16),
            vmem((32, 8, RANK), F32),
            vmem((31, 8, RANK), F32),
            vmem((2, 8, RANK), F32),
            vmem((7, 8, RANK), F32),
            vmem((32, 8, RANK), F32),
            vmem((RANK, RANK), F32),
            vmem((RANK, RANK), F32),
            vmem((2, 4, HALF, RANK), F32),
            vmem((4, HALF, RANK), F32),
            vmem((4, HALF, RANK), F32),
            vmem((3, HALF, RANK), F32),
            dma((SLOTS,)),
            dma((2,)),
            dma((2,)),
            dma((2, 2, 3)),
            dma((2, 2, 3)),
            dma((2, 2, 3)),
            dma((2, 2, 3)),
            dma,
            dma,
            dma((7,)),
            dma((7,)),
            dma,
            dma,
            dma,
            dma,
            dma((3,)),
            dma((3,)),
        ],
        compiler_params=pltpu.CompilerParams(
            collective_id=0, has_side_effects=True, vmem_limit_bytes=56 << 20
        ),
        cost_estimate=pl.CostEstimate(
            flops=3_300_000_000, bytes_accessed=12_000_000, transcendentals=0
        ),
    )(
        owner.reshape(SLOTS),
        sub_block,
        patient_block,
        live,
        tiles.reshape(SLOTS, BLOCK * MONTHS, BLOCK),
        code_factor,
        month_factor,
    )


def solution(mesh):
    placed = (
        P(("pat", "code"), None, None, None),
        P(("pat", "code")),
        P(("pat", "code"), None),
        P(("pat", "code")),
        P(("pat", "code")),
        P(("pat", "code"), None),
        P(),
    )
    return jax.shard_map(
        local, mesh=mesh, in_specs=placed, out_specs=P(("pat", "code"), None), check_vma=False
    )
```

time: 438 us -> 93.1 us (0.21)
  waiting for transfers between devices: 294 us -> 0 us
  Pallas kernels: 0 us -> 90.6 us
  other arithmetic: 54.5 us -> 0 us
  local copies, waits for them, and re-layouts: 36.1 us -> 1.47 us
  matrix products: 26.4 us -> 0 us
  between operations: 20.4 us -> 0.01 us
    psum x1 -> x0, waiting for transfers between devices: 285 us -> none  [local(): code_gram = lax.psum(local_gram, ('pat', 'code'))]
    pallas_call x0 -> x1, Pallas kernels: none -> 90.6 us  [local(): pl.pallas_call(kernel, out_shape=jax.ShapeDtypeStruct((HALF, RANK), F32),...]
    another operation x9 -> x0, other arithmetic: 53.7 us -> none  [the longest x6 34 us: local(): lower = jnp.linalg.cholesky(gram)]
    another operation x12 -> x0, local copies, waits for them, and re-layouts: 25.4 us -> none
    dot_general x5 -> x0, matrix products: 23.2 us -> none  [the longest x3 19.8 us: contract(): jnp.dot(counts_tile.reshape(block * months, block), code_block, preferred...]
    reduce_scatter x1 -> x0, waiting for transfers between devices: 7.95 us -> none  [local(): lax.psum_scatter(partial_rows, 'code', scatter_dimension=0, tiled=True)]
    slice x6 -> x0, local copies, waits for them, and re-layouts: 7.87 us -> none  [the longest x4 5.02 us: local(): start = (owner[index, 0] * own + sub_block[index]) * block]
  transfers between devices with their start and end apart: 3 -> 0, of which waited for: 2 -> 0; matrix products, arithmetic and copies ran while one was open for 15% -> 0% of each run, Pallas kernels for 0% -> 0%
where the time goes in v1:
time: 93.1 us; the launch traced here: 92 us
  Pallas kernels  90.6 us (97%)
  local copies, waits for them, and re-layouts  1.47 us (2%)
    pallas_call x1, Pallas kernels, local(): pl.pallas_call(kernel, out_shape=jax.ShapeDtypeStruct((HALF, RANK), F32),...  90.6 us

profile of v1, /device:TPU:1, one launch (start us, length us, event | category | flops | bytes accessed | tf_op | source)
XLA Modules:
  0.0 92.0 jit_solution(16395436999879225009)
XLA Ops:
  0.0 90.6 %shard_map.73 = f32[64,256]{1,0:T(8,128)} custom-call(s32[3]{0:T(128)} %bitcast.3, s32[3]{0:T(128)} %sub.1, s32[3]{0:T(128)} %block_at.1, s32[3]{0:T(128)} %live.1, bf16[3,15360,128]{2,1,0:T(8,128)(2,1)} %bitcast.2, bf16[256,256]{1,0:T(8,128)(2,1)} %code.1, f32[120,256]{1,0:T(8,128)} %month.1), custom_call_target="tpu_custom_call" | custom-call | flops 3300000000 | bytes 12000000 | tf_op jit(solution)/shard_map/pallas_call | solution.py:266
  90.6 1.5 %copy.9 = f32[64,256]{1,0:T(8,128)} copy(f32[64,256]{1,0:T(8,128)} %shard_map.73) | data formatting | bytes 131072

commit v2 on v1

v2 whole, which is shorter than its diff:
```python
import jax
import jax.numpy as jnp
from jax import lax
from jax.experimental import pallas as pl
from jax.experimental.pallas import tpu as pltpu
from jax.sharding import PartitionSpec as P

MESH = pl.DeviceIdType.MESH
HI = lax.Precision.HIGHEST
F32 = jnp.float32
BLOCK = 128
MONTHS = 120
RANK = 256
SLOTS = 3
HALF = 64
CHUNK = 32
SIDE = 32


def recip(p):
    r = pltpu.reciprocal(p, approx=True)
    return r * (2.0 - p * r)


def tree(values, bits):
    while len(values) > 1:
        values = [
            jnp.where(bits[0], values[i + 1], values[i]) for i in range(0, len(values), 2)
        ]
        bits = bits[1:]
    return values[0]


def add_up(values):
    while len(values) > 1:
        values = [values[i] + values[i + 1] for i in range(0, len(values), 2)]
    return values[0]


def lane_of(v, at):
    return jnp.broadcast_to(v[:, at : at + 1], (8, 128))


def row_of(v, at):
    return jnp.broadcast_to(v[at : at + 1, :], (8, 128))


def sweep_pairs(d):
    n = 8

    def at(i, j):
        return d[min(i, j), max(i, j)]

    for k in range(0, n, 2):
        a, b, c = at(k, k), at(k, k + 1), at(k + 1, k + 1)
        r = recip(a * c - b * b)
        ia, ib, ic = c * r, b * r, a * r
        rest = [i for i in range(n) if i > k + 1] + [i for i in range(n) if i < k]
        u = {
            i: (ia * at(k, i) - ib * at(k + 1, i), ic * at(k + 1, i) - ib * at(k, i)) for i in rest
        }
        new = {}
        for p, i in enumerate(rest):
            for j in rest[p:]:
                new[min(i, j), max(i, j)] = at(i, j) - (at(k, i) * u[j][0] + at(k + 1, i) * u[j][1])
        for i in rest:
            new[min(i, k), max(i, k)] = u[i][0]
            new[min(i, k + 1), max(i, k + 1)] = u[i][1]
        new[k, k], new[k, k + 1], new[k + 1, k + 1] = -ia, ib, -ic
        d = new
    return d


def panel(rows, half, l0, row, lane):
    c = [lane_of(rows[half], l0 + m) for m in range(8)]
    lines = [[row_of(rows[h], m) for m in range(8)] for h in range(2)]
    d = sweep_pairs({(i, j): row_of(c[j], i) for i in range(8) for j in range(i, 8)})
    row_bits = [(row & b) == b for b in (1, 2, 4)]
    rel = lane - l0
    lane_bits = [(rel & b) == b for b in (1, 2, 4)]
    minus = [tree([d[min(i, m), max(i, m)] for i in range(8)], row_bits) for m in range(8)]
    inside = -tree(minus, lane_bits)
    out = []
    for h in range(2):
        w = -add_up([minus[m] * lines[h][m] for m in range(8)])
        out.append(jnp.where((rel >= 0) & (rel < 8), inside, w) if h == half else w)
    return out


def turned_dot(a, b):
    return lax.dot_general(
        a, b, (((0,), (0,)), ((), ())), precision=HI, preferred_element_type=F32
    )


def clear_and_subtract(a, s, rows, done):
    wide = lax.broadcasted_iota(jnp.int32, (1, RANK), 1)
    o = s * SIDE
    inside = (wide >= o) & (wide < o + SIDE)
    a[...] = jnp.where(inside, 0.0, a[...]) - turned_dot(rows, done)
    a[pl.ds(pl.multiple_of(jnp.maximum(o, 0), SIDE), SIDE), :] = done


def eliminate(a, first, last, carry):
    row = lax.broadcasted_iota(jnp.int32, (8, 128), 0)
    lane = lax.broadcasted_iota(jnp.int32, (8, 128), 1)
    wide = lax.broadcasted_iota(jnp.int32, (1, RANK), 1)
    n = SIDE // 8

    def step(s, carry):
        turned, before, after = carry
        clear_and_subtract(a, s - 1, before, after)
        o = pl.multiple_of(s * SIDE, SIDE)
        ahead = pl.multiple_of(lax.rem(o + SIDE, RANK), SIDE)
        following = pltpu.roll(a[pl.ds(ahead, SIDE), :], RANK - o, 1)
        straight = pltpu.roll(turned, o, 1)
        rows = [[turned[8 * j : 8 * j + 8, :128], turned[8 * j : 8 * j + 8, 128:]] for j in range(n)]
        for j in range(n):
            l0 = 8 * j
            order = list(range(j + 1, n)) + list(range(j))
            factor = {i: [lane_of(rows[i][0], l0 + m) for m in range(8)] for i in order}
            rows[j] = panel(rows[j], 0, l0, row, lane)
            inside = (lane >= l0) & (lane < l0 + 8)
            w = [[row_of(rows[j][h], m) for m in range(8)] for h in range(2)]
            for i in order:
                for h in range(2):
                    old = jnp.where(inside, 0.0, rows[i][h]) if h == 0 else rows[i][h]
                    rows[i][h] = old - add_up([factor[i][m] * w[h][m] for m in range(8)])
        done = jnp.concatenate([jnp.concatenate(r, axis=1) for r in rows], axis=0)
        done = jnp.where(wide < SIDE, -done, done)
        following = jnp.where(wide < SIDE, 0.0, following) - turned_dot(
            turned[:, SIDE : 2 * SIDE], done
        )
        return pltpu.roll(following, RANK - SIDE, 1), straight, pltpu.roll(done, o, 1)

    return lax.fori_loop(first, last, step, carry)


def kernel(
    owner, sub, block_at, live, tiles, code_in, month_in, out,
    counts, code, month, group, need, need_in, asked, wanted, chosen, blocks,
    gram_own, plane_in, piece, column_in, whole, gram, month_gram,
    part, pair_in, line_out, line_in,
    tile_sem, small_sem, need_s, need_r, asked_sem, zh_s, zh_r, row_s, row_r, pick_s, pick_r,
    plane_s, plane_r, column_s, column_r, spread_s, spread_r,
    pair_s, pair_r, line_s, line_r,
):
    pat, code_at = lax.axis_index("pat"), lax.axis_index("code")
    x, y, zh = pat // 8, (pat // 2) % 4, pat % 2
    zl, core = code_at // 2, code_at % 2
    z = zh * 4 + zl
    me = (x * 4 + y) * 2 + core

    def device(x, y, z, c):
        x, y, z = lax.rem(x, 4), lax.rem(y, 4), lax.rem(z, 8)
        return ((x * 4 + y) * 2 + z // 4, lax.rem(z, 4) * 2 + c)

    def plane(e):
        px, py, pc = lax.rem(x + e // 8, 4), lax.rem(y + (e // 2) % 4, 4), lax.rem(core + e % 2, 2)
        return device(px, py, z, pc), (px * 4 + py) * 2 + pc

    def beside(h, d):
        return device(x + d, y, z, core) if h == 0 else device(x, y + d, z, core)

    def remote(src, dst, send, recv, to):
        return pltpu.make_async_remote_copy(
            src_ref=src, dst_ref=dst, send_sem=send, recv_sem=recv, device_id=to, device_id_type=MESH
        )

    def start(copies):
        for c in copies:
            c.start()
        return copies

    def arrived(buf, sem):
        pltpu.make_async_copy(buf, buf, sem).wait()

    small = start(
        [
            pltpu.make_async_copy(code_in, code, small_sem.at[0]),
            pltpu.make_async_copy(month_in, month, small_sem.at[1]),
        ]
    )
    loads = start(
        [pltpu.make_async_copy(tiles.at[k], counts.at[k], tile_sem.at[k]) for k in range(SLOTS)]
    )
    barrier = pltpu.get_barrier_semaphore()

    def greet(e, _):
        pl.semaphore_signal(barrier, inc=1, device_id=plane(e)[0], device_id_type=MESH)
        return 0

    lax.fori_loop(1, 32, greet, 0)
    for d in range(1, 8):
        pl.semaphore_signal(
            barrier, inc=1, device_id=device(x, y, z + d, core), device_id_type=MESH
        )
    line_at = lax.broadcasted_iota(jnp.int32, (8, 128), 0)
    places, away = [], []
    for k in range(SLOTS):
        o = owner[k]
        ox, oy, oz = o // 8, (o // 2) % 4, o % 2
        places.append([(oz * 4 + ox) * 2 + sub[k], (oz * 4 + oy) * 2 + sub[k]])
        away.append([lax.rem(y + 4 - oy, 4), lax.rem(x + 4 - ox, 4)])
    wish = jnp.zeros((8, 128), jnp.int32)
    for k in range(SLOTS):
        for h in range(2):
            wish = jnp.where(line_at == 2 * k + h, places[k][h], wish)
    need[...] = wish
    mine = [(zh * 4 + x) * 2, (zh * 4 + y) * 2]
    theirs = [((1 - zh) * 4 + x) * 2, ((1 - zh) * 4 + y) * 2]
    small[0].wait()
    for h in range(2):
        for b in range(2):
            group[h, mine[h] + b] = code[b * BLOCK : (b + 1) * BLOCK, h * BLOCK : (h + 1) * BLOCK]
    own = lax.dot_general(
        code[...], code[...], (((0,), (0,)), ((), ())), preferred_element_type=F32
    )
    gram_own[...] = own.reshape(32, 8, RANK)
    pl.semaphore_wait(barrier, 38)

    across = []
    for h in range(2):
        here = group.at[h, pl.ds(mine[h], 2)]
        across.append(remote(here, here, zh_s.at[h], zh_r.at[h], device(x, y, z + 4, core)))
    start(across)
    needs = start(
        [
            remote(need, need_in.at[h, d - 1], need_s.at[h, d - 1], need_r.at[h, d - 1], beside(1 - h, d))
            for h in range(2)
            for d in range(1, 4)
        ]
    )

    def scatter(e, _):
        to, q = plane(e)
        remote(gram_own.at[q], plane_in.at[e - 1], plane_s, plane_r, to).start()
        return 0

    lax.fori_loop(1, 32, scatter, 0)

    def along_line(s, first):
        copies = []
        for h in range(2):
            here = group.at[h, pl.ds(first[h], 2)]
            for d in range(1, 4):
                copies.append(
                    remote(here, here, row_s.at[s, h, d - 1], row_r.at[s, h, d - 1], beside(h, d))
                )
        return start(copies)

    row_copies = along_line(0, mine)
    small[1].wait()
    month_gram[...] = turned_dot(month[...], month[...])
    for c in needs:
        c.wait()
    to_scalars = pltpu.make_async_copy(need_in, asked, asked_sem)
    to_scalars.start()
    to_scalars.wait()
    arrived(plane_in, plane_r)

    def add_plane(e, total):
        return total + plane_in[e]

    piece[0] = lax.fori_loop(0, 31, add_plane, gram_own[me], unroll=True)
    columns = start(
        [
            remote(
                piece.at[0], column_in.at[d - 1], column_s.at[d - 1], column_r.at[d - 1],
                device(x, y, z + d, core),
            )
            for d in range(1, 8)
        ]
    )
    for c in across:
        c.wait()
    row_copies = row_copies + along_line(1, theirs)
    for c in row_copies:
        c.wait()
    picks = []
    for k in range(SLOTS):
        for h in range(2):
            for d in range(1, 4):
                wanted[k, h, d - 1] = group[h, asked[h, 3 - d, 2 * k + h, 0]]
                picks.append(
                    remote(
                        wanted.at[k, h, d - 1], chosen.at[k, h, d],
                        pick_s.at[k, h, d - 1], pick_r.at[k, h, d - 1], beside(1 - h, d),
                    )
                )
                picks[-1].start()
            chosen[k, h, 0] = group[h, places[k][h]]
    for c in columns:
        c.wait()
    total = piece[0]
    for d in range(7):
        total = total + column_in[d]
    piece[1] = total
    whole[me] = total

    def spread(e, _):
        to, _q = plane(e)
        remote(piece.at[1], whole.at[me], spread_s, spread_r, to).start()
        return 0

    lax.fori_loop(1, 32, spread, 0)
    for c in picks:
        c.wait()
    for k in range(SLOTS):
        for h in range(2):
            blocks[k, :, h * BLOCK : (h + 1) * BLOCK] = chosen[k, h, away[k][h]]
    for load in loads:
        load.wait()

    def contract(half, low):
        pieces = []
        for k in range(SLOTS):
            at = pl.multiple_of((half * HALF + low) * MONTHS, CHUNK * MONTHS)
            wide = jnp.dot(
                counts[k, pl.ds(at, CHUNK * MONTHS), :], blocks[k], preferred_element_type=F32
            )
            wide = wide.reshape(CHUNK, MONTHS, RANK) * month[...][None]
            pieces.append(jnp.sum(wide, axis=1) * live[k].astype(F32))
        for b in range(4):
            part[half, b, pl.ds(low, CHUNK), :] = add_three(
                [jnp.where(block_at[k] == b, pieces[k], 0.0) for k in range(SLOTS)]
            )

    def add_three(v):
        return v[0] + v[1] + v[2]

    pairs, line = [], []
    for which in range(2):
        half = 1 - core if which == 0 else core
        for n in range(HALF // CHUNK):
            at = pl.ds(n * CHUNK, CHUNK)
            contract(half, n * CHUNK)
            if which == 0:
                pairs.append(
                    remote(
                        part.at[half, :, at], pair_in.at[:, at], pair_s.at[n], pair_r.at[n],
                        device(x, y, z, 1 - core),
                    )
                )
                pairs[-1].start()
            else:
                pairs[n].wait()
                line_out[:, at] = part[half, :, at] + pair_in[:, at]
                for d in range(1, 4):
                    zt = lax.rem(zl + d, 4)
                    line.append(
                        remote(
                            line_out.at[zt, at], line_in.at[d - 1, at],
                            line_s.at[n, d - 1], line_r.at[n, d - 1], device(x, y, zh * 4 + zt, core),
                        )
                    )
                    line[-1].start()
    arrived(whole.at[0:31], spread_r)
    gram[...] = whole[...].reshape(RANK, RANK) * month_gram[...]
    first = gram[0:SIDE, :]
    _, before, after = eliminate(
        gram, 0, RANK // SIDE, (first, jnp.zeros_like(first), first)
    )
    clear_and_subtract(gram, RANK // SIDE - 1, before, after)
    for c in line:
        c.wait()
    share = line_out[zl] + line_in[0] + line_in[1] + line_in[2]
    out[...] = -jnp.dot(share, gram[...], precision=HI, preferred_element_type=F32)
    arrived(gram_own.at[0:31], plane_s)
    arrived(gram_own.at[0:31], spread_s)


def local(tiles, patient_block, owner, sub_block, live, code_factor, month_factor):
    dma, vmem = pltpu.SemaphoreType.DMA, pltpu.VMEM
    smem_spec = pl.BlockSpec(memory_space=pltpu.SMEM)
    vmem_spec = pl.BlockSpec(memory_space=pltpu.VMEM)
    return pl.pallas_call(
        kernel,
        out_shape=jax.ShapeDtypeStruct((HALF, RANK), F32),
        in_specs=[smem_spec] * 4 + [pl.BlockSpec(memory_space=pl.ANY)] * 3,
        out_specs=vmem_spec,
        scratch_shapes=[
            vmem((SLOTS, BLOCK * MONTHS, BLOCK), jnp.bfloat16),
            vmem((2 * BLOCK, RANK), jnp.bfloat16),
            vmem((MONTHS, RANK), F32),
            vmem((2, 16, BLOCK, BLOCK), jnp.bfloat16),
            vmem((8, 128), jnp.int32),
            vmem((2, 3, 8, 128), jnp.int32),
            pltpu.SMEM((2, 3, 8, 128), jnp.int32),
            vmem((SLOTS, 2, 3, BLOCK, BLOCK), jnp.bfloat16),
            vmem((SLOTS, 2, 4, BLOCK, BLOCK), jnp.bfloat16),
            vmem((SLOTS, BLOCK, RANK), jnp.bfloat16),
            vmem((32, 8, RANK), F32),
            vmem((31, 8, RANK), F32),
            vmem((2, 8, RANK), F32),
            vmem((7, 8, RANK), F32),
            vmem((32, 8, RANK), F32),
            vmem((RANK, RANK), F32),
            vmem((RANK, RANK), F32),
            vmem((2, 4, HALF, RANK), F32),
            vmem((4, HALF, RANK), F32),
            vmem((4, HALF, RANK), F32),
            vmem((3, HALF, RANK), F32),
            dma((SLOTS,)),
            dma((2,)),
            dma((2, 3)),
            dma((2, 3)),
            dma,
            dma((2,)),
            dma((2,)),
            dma((2, 2, 3)),
            dma((2, 2, 3)),
            dma((SLOTS, 2, 3)),
            dma((SLOTS, 2, 3)),
            dma,
            dma,
            dma((7,)),
            dma((7,)),
            dma,
            dma,
            dma((HALF // CHUNK,)),
            dma((HALF // CHUNK,)),
            dma((HALF // CHUNK, 3)),
            dma((HALF // CHUNK, 3)),
        ],
        compiler_params=pltpu.CompilerParams(
            collective_id=0, has_side_effects=True, vmem_limit_bytes=56 << 20
        ),
        cost_estimate=pl.CostEstimate(
            flops=3_300_000_000, bytes_accessed=12_000_000, transcendentals=0
        ),
    )(
        owner.reshape(SLOTS),
        sub_block,
        patient_block,
        live,
        tiles.reshape(SLOTS, BLOCK * MONTHS, BLOCK),
        code_factor,
        month_factor,
    )


def solution(mesh):
    placed = (
        P(("pat", "code"), None, None, None),
        P(("pat", "code")),
        P(("pat", "code"), None),
        P(("pat", "code")),
        P(("pat", "code")),
        P(("pat", "code"), None),
        P(),
    )
    return jax.shard_map(
        local, mesh=mesh, in_specs=placed, out_specs=P(("pat", "code"), None), check_vma=False
    )
```

time: 93.1 us -> 57.5 us (0.62)
  the two profiles are of different devices: /device:TPU:1 before, /device:TPU:32 now
where the time goes in v2:
time: 57.5 us; the launch traced here: 57.4 us
  Pallas kernels  55.9 us (97%)
  local copies, waits for them, and re-layouts  1.47 us (3%)
    pallas_call x1, Pallas kernels, local(): pl.pallas_call(kernel, out_shape=jax.ShapeDtypeStruct((HALF, RANK), F32),...  55.9 us
    unnamed x1, local copies, waits for them, and re-layouts  1.47 us

profile of v2, /device:TPU:32, one launch (start us, length us, event | category | flops | bytes accessed | tf_op | source)
XLA Modules:
  0.0 57.4 jit_solution(17645206810690912544)
XLA Ops:
  0.0 55.9 %shard_map.73 = f32[64,256]{1,0:T(8,128)} custom-call(s32[3]{0:T(128)} %bitcast.3, s32[3]{0:T(128)} %sub.1, s32[3]{0:T(128)} %block_at.1, s32[3]{0:T(128)} %live.1, bf16[3,15360,128]{2,1,0:T(8,128)(2,1)} %bitcast.2, bf16[256,256]{1,0:T(8,128)(2,1)} %code_in.1, f32[120,256]{1,0:T(8,128)} %month_in.1), custom_call_target="tpu_custom_call" | custom-call | flops 3300000000 | bytes 12000000 | tf_op jit(solution)/shard_map/pallas_call | solution.py:377
  55.9 1.5 %copy.9 = f32[64,256]{1,0:T(8,128)} copy(f32[64,256]{1,0:T(8,128)} %shard_map.73) | data formatting | bytes 131072

commit v3 on v2

--- a/solution.py
+++ b/solution.py
@@ -101,7 +101,7 @@
     a[pl.ds(pl.multiple_of(jnp.maximum(o, 0), SIDE), SIDE), :] = done
 
 
-def eliminate(a, first, last, carry):
+def eliminate(a, first, last, carry, beside=None, after_step=None):
     row = lax.broadcasted_iota(jnp.int32, (8, 128), 0)
     lane = lax.broadcasted_iota(jnp.int32, (8, 128), 1)
     wide = lax.broadcasted_iota(jnp.int32, (1, RANK), 1)
@@ -119,6 +119,8 @@
             l0 = 8 * j
             order = list(range(j + 1, n)) + list(range(j))
             factor = {i: [lane_of(rows[i][0], l0 + m) for m in range(8)] for i in order}
+            if beside is not None and j == 1:
+                beside(s)
             rows[j] = panel(rows[j], 0, l0, row, lane)
             inside = (lane >= l0) & (lane < l0 + 8)
             w = [[row_of(rows[j][h], m) for m in range(8)] for h in range(2)]
@@ -131,7 +133,10 @@
         following = jnp.where(wide < SIDE, 0.0, following) - turned_dot(
             turned[:, SIDE : 2 * SIDE], done
         )
-        return pltpu.roll(following, RANK - SIDE, 1), straight, pltpu.roll(done, o, 1)
+        result = pltpu.roll(following, RANK - SIDE, 1), straight, pltpu.roll(done, o, 1)
+        if after_step is not None:
+            after_step(s)
+        return result
 
     return lax.fori_loop(first, last, step, carry)
 
@@ -142,14 +147,15 @@
     gram_own, plane_in, piece, column_in, whole, gram, month_gram,
     part, pair_in, line_out, line_in,
     tile_sem, small_sem, need_s, need_r, asked_sem, zh_s, zh_r, row_s, row_r, pick_s, pick_r,
-    plane_s, plane_r, column_s, column_r, spread_s, spread_r,
+    plane_s, plane_r, column_s, column_r, spread_s, spread_r, halves_s, halves_r,
     pair_s, pair_r, line_s, line_r,
 ):
     pat, code_at = lax.axis_index("pat"), lax.axis_index("code")
     x, y, zh = pat // 8, (pat // 2) % 4, pat % 2
     zl, core = code_at // 2, code_at % 2
     z = zh * 4 + zl
-    me = (x * 4 + y) * 2 + core
+    spot = x * 4 + y
+    me = core * 16 + spot
 
     def device(x, y, z, c):
         x, y, z = lax.rem(x, 4), lax.rem(y, 4), lax.rem(z, 8)
@@ -157,7 +163,7 @@
 
     def plane(e):
         px, py, pc = lax.rem(x + e // 8, 4), lax.rem(y + (e // 2) % 4, 4), lax.rem(core + e % 2, 2)
-        return device(px, py, z, pc), (px * 4 + py) * 2 + pc
+        return device(px, py, z, pc), pc * 16 + px * 4 + py
 
     def beside(h, d):
         return device(x + d, y, z, core) if h == 0 else device(x, y + d, z, core)
@@ -190,11 +196,11 @@
         pl.semaphore_signal(barrier, inc=1, device_id=plane(e)[0], device_id_type=MESH)
         return 0
 
-    lax.fori_loop(1, 32, greet, 0)
-    for d in range(1, 8):
+    for d in (4, 3, 5, 2, 6, 1, 7):
         pl.semaphore_signal(
             barrier, inc=1, device_id=device(x, y, z + d, core), device_id_type=MESH
         )
+    lax.fori_loop(1, 32, greet, 0)
     line_at = lax.broadcasted_iota(jnp.int32, (8, 128), 0)
     places, away = [], []
     for k in range(SLOTS):
@@ -213,16 +219,13 @@
     for h in range(2):
         for b in range(2):
             group[h, mine[h] + b] = code[b * BLOCK : (b + 1) * BLOCK, h * BLOCK : (h + 1) * BLOCK]
-    own = lax.dot_general(
-        code[...], code[...], (((0,), (0,)), ((), ())), preferred_element_type=F32
-    )
-    gram_own[...] = own.reshape(32, 8, RANK)
     pl.semaphore_wait(barrier, 38)
 
     across = []
-    for h in range(2):
-        here = group.at[h, pl.ds(mine[h], 2)]
-        across.append(remote(here, here, zh_s.at[h], zh_r.at[h], device(x, y, z + 4, core)))
+    for b in range(2):
+        for h in range(2):
+            here = group.at[h, mine[h] + b]
+            across.append(remote(here, here, zh_s.at[b, h], zh_r.at[b, h], device(x, y, z + 4, core)))
     start(across)
     needs = start(
         [
@@ -232,6 +235,11 @@
         ]
     )
 
+    own = lax.dot_general(
+        code[...], code[...], (((0,), (0,)), ((), ())), preferred_element_type=F32
+    )
+    gram_own[...] = own.reshape(32, 8, RANK)
+
     def scatter(e, _):
         to, q = plane(e)
         remote(gram_own.at[q], plane_in.at[e - 1], plane_s, plane_r, to).start()
@@ -239,17 +247,17 @@
 
     lax.fori_loop(1, 32, scatter, 0)
 
-    def along_line(s, first):
+    def along_line(s, first, count):
         copies = []
         for h in range(2):
-            here = group.at[h, pl.ds(first[h], 2)]
+            here = group.at[h, pl.ds(first[h], count)]
             for d in range(1, 4):
                 copies.append(
                     remote(here, here, row_s.at[s, h, d - 1], row_r.at[s, h, d - 1], beside(h, d))
                 )
         return start(copies)
 
-    row_copies = along_line(0, mine)
+    row_copies = along_line(0, mine, 2)
     small[1].wait()
     month_gram[...] = turned_dot(month[...], month[...])
     for c in needs:
@@ -257,12 +265,11 @@
     to_scalars = pltpu.make_async_copy(need_in, asked, asked_sem)
     to_scalars.start()
     to_scalars.wait()
+    for c in across[:2]:
+        c.wait()
+    row_copies = row_copies + along_line(1, theirs, 1)
     arrived(plane_in, plane_r)
-
-    def add_plane(e, total):
-        return total + plane_in[e]
-
-    piece[0] = lax.fori_loop(0, 31, add_plane, gram_own[me], unroll=True)
+    piece[0] = lax.fori_loop(0, 31, lambda e, t: t + plane_in[e], gram_own[me], unroll=True)
     columns = start(
         [
             remote(
@@ -272,9 +279,23 @@
             for d in range(1, 8)
         ]
     )
-    for c in across:
-        c.wait()
-    row_copies = row_copies + along_line(1, theirs)
+    for c in across[2:]:
+        c.wait()
+    row_copies = row_copies + along_line(2, [t + 1 for t in theirs], 1)
+    for c in columns:
+        c.wait()
+    total = piece[0]
+    for d in range(7):
+        total = total + column_in[d]
+    piece[1] = total
+    whole[core, spot] = total
+
+    def spread(e, _):
+        to = device(x + e // 4, y + e % 4, z, core)
+        remote(piece.at[1], whole.at[core, spot], spread_s, spread_r, to).start()
+        return 0
+
+    lax.fori_loop(1, 16, spread, 0)
     for c in row_copies:
         c.wait()
     picks = []
@@ -290,20 +311,14 @@
                 )
                 picks[-1].start()
             chosen[k, h, 0] = group[h, places[k][h]]
-    for c in columns:
-        c.wait()
-    total = piece[0]
-    for d in range(7):
-        total = total + column_in[d]
-    piece[1] = total
-    whole[me] = total
-
-    def spread(e, _):
-        to, _q = plane(e)
-        remote(piece.at[1], whole.at[me], spread_s, spread_r, to).start()
-        return 0
-
-    lax.fori_loop(1, 32, spread, 0)
+    arrived(whole.at[0, 0:15], spread_r)
+    halves = remote(
+        whole.at[core], whole.at[core], halves_s, halves_r, device(x, y, z, 1 - core)
+    )
+    halves.start()
+    halves.wait()
+    gram[...] = whole[...].reshape(RANK, RANK) * month_gram[...]
+    first = gram[0:SIDE, :]
     for c in picks:
         c.wait()
     for k in range(SLOTS):
@@ -312,62 +327,63 @@
     for load in loads:
         load.wait()
 
-    def contract(half, low):
+    per_half = HALF // CHUNK
+
+    def contract(s):
+        half = jnp.where(s < per_half, 1 - core, core)
+        low = pl.multiple_of(lax.rem(s, per_half) * CHUNK, CHUNK)
+        at = pl.multiple_of((half * HALF + low) * MONTHS, CHUNK * MONTHS)
         pieces = []
         for k in range(SLOTS):
-            at = pl.multiple_of((half * HALF + low) * MONTHS, CHUNK * MONTHS)
             wide = jnp.dot(
                 counts[k, pl.ds(at, CHUNK * MONTHS), :], blocks[k], preferred_element_type=F32
             )
             wide = wide.reshape(CHUNK, MONTHS, RANK) * month[...][None]
             pieces.append(jnp.sum(wide, axis=1) * live[k].astype(F32))
         for b in range(4):
-            part[half, b, pl.ds(low, CHUNK), :] = add_three(
-                [jnp.where(block_at[k] == b, pieces[k], 0.0) for k in range(SLOTS)]
-            )
-
-    def add_three(v):
-        return v[0] + v[1] + v[2]
-
-    pairs, line = [], []
-    for which in range(2):
-        half = 1 - core if which == 0 else core
-        for n in range(HALF // CHUNK):
-            at = pl.ds(n * CHUNK, CHUNK)
-            contract(half, n * CHUNK)
-            if which == 0:
-                pairs.append(
-                    remote(
-                        part.at[half, :, at], pair_in.at[:, at], pair_s.at[n], pair_r.at[n],
-                        device(x, y, z, 1 - core),
-                    )
-                )
-                pairs[-1].start()
-            else:
-                pairs[n].wait()
-                line_out[:, at] = part[half, :, at] + pair_in[:, at]
-                for d in range(1, 4):
-                    zt = lax.rem(zl + d, 4)
-                    line.append(
-                        remote(
-                            line_out.at[zt, at], line_in.at[d - 1, at],
-                            line_s.at[n, d - 1], line_r.at[n, d - 1], device(x, y, zh * 4 + zt, core),
-                        )
-                    )
-                    line[-1].start()
-    arrived(whole.at[0:31], spread_r)
-    gram[...] = whole[...].reshape(RANK, RANK) * month_gram[...]
-    first = gram[0:SIDE, :]
-    _, before, after = eliminate(
-        gram, 0, RANK // SIDE, (first, jnp.zeros_like(first), first)
-    )
+            chosen_pieces = [jnp.where(block_at[k] == b, pieces[k], 0.0) for k in range(SLOTS)]
+            part[half, b, pl.ds(low, CHUNK), :] = chosen_pieces[0] + chosen_pieces[1] + chosen_pieces[2]
+
+    def pair_copy(n):
+        at = pl.ds(pl.multiple_of(n * CHUNK, CHUNK), CHUNK)
+        return remote(
+            part.at[1 - core, :, at], pair_in.at[:, at], pair_s.at[n], pair_r.at[n],
+            device(x, y, z, 1 - core),
+        )
+
+    def line_copy(n, d):
+        at = pl.ds(pl.multiple_of(n * CHUNK, CHUNK), CHUNK)
+        zt = lax.rem(zl + d, 4)
+        return remote(
+            line_out.at[zt, at], line_in.at[d - 1, at], line_s.at[n, d - 1], line_r.at[n, d - 1],
+            device(x, y, zh * 4 + zt, core),
+        )
+
+    def send_sums(s):
+        @pl.when(s < per_half)
+        def _():
+            pair_copy(s).start()
+
+        @pl.when(s >= per_half)
+        def _():
+            n = s - per_half
+            at = pl.ds(pl.multiple_of(n * CHUNK, CHUNK), CHUNK)
+            pair_copy(n).wait()
+            line_out[:, at] = part[core, :, at] + pair_in[:, at]
+            for d in range(1, 4):
+                line_copy(n, d).start()
+
+    carry = (first, jnp.zeros_like(first), first)
+    carry = eliminate(gram, 0, 2 * per_half, carry, contract, send_sums)
+    line = [line_copy(n, d) for n in range(per_half) for d in range(1, 4)]
+    _, before, after = eliminate(gram, 2 * per_half, RANK // SIDE, carry)
     clear_and_subtract(gram, RANK // SIDE - 1, before, after)
     for c in line:
         c.wait()
     share = line_out[zl] + line_in[0] + line_in[1] + line_in[2]
     out[...] = -jnp.dot(share, gram[...], precision=HI, preferred_element_type=F32)
     arrived(gram_own.at[0:31], plane_s)
-    arrived(gram_own.at[0:31], spread_s)
+    arrived(gram_own.at[0:15], spread_s)
 
 
 def local(tiles, patient_block, owner, sub_block, live, code_factor, month_factor):
@@ -394,7 +410,7 @@
             vmem((31, 8, RANK), F32),
             vmem((2, 8, RANK), F32),
             vmem((7, 8, RANK), F32),
-            vmem((32, 8, RANK), F32),
+            vmem((2, 16, 8, RANK), F32),
             vmem((RANK, RANK), F32),
             vmem((RANK, RANK), F32),
             vmem((2, 4, HALF, RANK), F32),
@@ -406,16 +422,18 @@
             dma((2, 3)),
             dma((2, 3)),
             dma,
-            dma((2,)),
-            dma((2,)),
-            dma((2, 2, 3)),
-            dma((2, 2, 3)),
+            dma((2, 2)),
+            dma((2, 2)),
+            dma((3, 2, 3)),
+            dma((3, 2, 3)),
             dma((SLOTS, 2, 3)),
             dma((SLOTS, 2, 3)),
             dma,
             dma,
             dma((7,)),
             dma((7,)),
+            dma,
+            dma,
             dma,
             dma,
             dma((HALF // CHUNK,)),

time: 57.5 us -> 52.1 us (0.906)
  the two profiles are of different devices: /device:TPU:32 before, /device:TPU:1 now
where the time goes in v3:
time: 52.1 us; the launch traced here: 52 us
  Pallas kernels  50.5 us (97%)
  local copies, waits for them, and re-layouts  1.47 us (3%)
    pallas_call x1, Pallas kernels, local(): pl.pallas_call(kernel, out_shape=jax.ShapeDtypeStruct((HALF, RANK), F32),...  50.5 us
    unnamed x1, local copies, waits for them, and re-layouts  1.47 us

profile of v3, /device:TPU:1, one launch (start us, length us, event | category | flops | bytes accessed | tf_op | source)
XLA Modules:
  0.0 52.0 jit_solution(927350422671669678)
XLA Ops:
  0.0 50.5 %shard_map.73 = f32[64,256]{1,0:T(8,128)} custom-call(s32[3]{0:T(128)} %bitcast.3, s32[3]{0:T(128)} %sub.1, s32[3]{0:T(128)} %block_at.1, s32[3]{0:T(128)} %live.1, bf16[3,15360,128]{2,1,0:T(8,128)(2,1)} %bitcast.2, bf16[256,256]{1,0:T(8,128)(2,1)} %code_in.1, f32[120,256]{1,0:T(8,128)} %month_in.1), custom_call_target="tpu_custom_call" | custom-call | flops 3300000000 | bytes 12000000 | tf_op jit(solution)/shard_map/pallas_call | solution.py:393
  50.5 1.5 %copy.9 = f32[64,256]{1,0:T(8,128)} copy(f32[64,256]{1,0:T(8,128)} %shard_map.73) | data formatting | bytes 131072

commit v4 on v3

--- a/solution.py
+++ b/solution.py
@@ -141,12 +141,23 @@
     return lax.fori_loop(first, last, step, carry)
 
 
+def far_first(offsets, hops):
+    return sorted(offsets, key=hops, reverse=True)
+
+
+RING = (0, 1, 2, 1)
+PLANE = far_first(range(1, 32), lambda e: RING[e // 8] + RING[e // 2 % 4])
+SPOTS = far_first(range(1, 16), lambda e: RING[e // 4] + RING[e % 4])
+COLUMN = far_first(range(1, 8), lambda d: min(d, 8 - d))
+LINE = (2, 1, 3)
+
+
 def kernel(
-    owner, sub, block_at, live, tiles, code_in, month_in, out,
+    owner_in, sub_in, block_in, live_in, tiles, code_in, month_in, out, owner, sub, block_at, live,
     counts, code, month, group, need, need_in, asked, wanted, chosen, blocks,
     gram_own, plane_in, piece, column_in, whole, gram, month_gram,
     part, pair_in, line_out, line_in,
-    tile_sem, small_sem, need_s, need_r, asked_sem, zh_s, zh_r, row_s, row_r, pick_s, pick_r,
+    scalar_sem, tile_sem, small_sem, need_s, need_r, asked_sem, zh_s, zh_r, row_s, row_r, pick_s, pick_r,
     plane_s, plane_r, column_s, column_r, spread_s, spread_r, halves_s, halves_r,
     pair_s, pair_r, line_s, line_r,
 ):
@@ -162,7 +173,9 @@
         return ((x * 4 + y) * 2 + z // 4, lax.rem(z, 4) * 2 + c)
 
     def plane(e):
-        px, py, pc = lax.rem(x + e // 8, 4), lax.rem(y + (e // 2) % 4, 4), lax.rem(core + e % 2, 2)
+        px, py, pc = lax.rem(x + e // 8, 4), lax.rem(y + (e // 2) % 4, 4), core
+        if e % 2:
+            pc = 1 - core
         return device(px, py, z, pc), pc * 16 + px * 4 + py
 
     def beside(h, d):
@@ -190,17 +203,24 @@
     loads = start(
         [pltpu.make_async_copy(tiles.at[k], counts.at[k], tile_sem.at[k]) for k in range(SLOTS)]
     )
+    scalars = start(
+        [
+            pltpu.make_async_copy(src, dst, scalar_sem.at[n])
+            for n, (src, dst) in enumerate(
+                ((owner_in, owner), (sub_in, sub), (block_in, block_at), (live_in, live))
+            )
+        ]
+    )
     barrier = pltpu.get_barrier_semaphore()
 
-    def greet(e, _):
-        pl.semaphore_signal(barrier, inc=1, device_id=plane(e)[0], device_id_type=MESH)
-        return 0
-
-    for d in (4, 3, 5, 2, 6, 1, 7):
+    for d in COLUMN:
         pl.semaphore_signal(
             barrier, inc=1, device_id=device(x, y, z + d, core), device_id_type=MESH
         )
-    lax.fori_loop(1, 32, greet, 0)
+    for e in PLANE:
+        pl.semaphore_signal(barrier, inc=1, device_id=plane(e)[0], device_id_type=MESH)
+    for c in scalars:
+        c.wait()
     line_at = lax.broadcasted_iota(jnp.int32, (8, 128), 0)
     places, away = [], []
     for k in range(SLOTS):
@@ -240,18 +260,15 @@
     )
     gram_own[...] = own.reshape(32, 8, RANK)
 
-    def scatter(e, _):
+    for e in PLANE:
         to, q = plane(e)
         remote(gram_own.at[q], plane_in.at[e - 1], plane_s, plane_r, to).start()
-        return 0
-
-    lax.fori_loop(1, 32, scatter, 0)
 
     def along_line(s, first, count):
         copies = []
         for h in range(2):
             here = group.at[h, pl.ds(first[h], count)]
-            for d in range(1, 4):
+            for d in LINE:
                 copies.append(
                     remote(here, here, row_s.at[s, h, d - 1], row_r.at[s, h, d - 1], beside(h, d))
                 )
@@ -276,7 +293,7 @@
                 piece.at[0], column_in.at[d - 1], column_s.at[d - 1], column_r.at[d - 1],
                 device(x, y, z + d, core),
             )
-            for d in range(1, 8)
+            for d in COLUMN
         ]
     )
     for c in across[2:]:
@@ -290,18 +307,15 @@
     piece[1] = total
     whole[core, spot] = total
 
-    def spread(e, _):
+    for e in SPOTS:
         to = device(x + e // 4, y + e % 4, z, core)
         remote(piece.at[1], whole.at[core, spot], spread_s, spread_r, to).start()
-        return 0
-
-    lax.fori_loop(1, 16, spread, 0)
     for c in row_copies:
         c.wait()
     picks = []
     for k in range(SLOTS):
         for h in range(2):
-            for d in range(1, 4):
+            for d in LINE:
                 wanted[k, h, d - 1] = group[h, asked[h, 3 - d, 2 * k + h, 0]]
                 picks.append(
                     remote(
@@ -388,14 +402,14 @@
 
 def local(tiles, patient_block, owner, sub_block, live, code_factor, month_factor):
     dma, vmem = pltpu.SemaphoreType.DMA, pltpu.VMEM
-    smem_spec = pl.BlockSpec(memory_space=pltpu.SMEM)
     vmem_spec = pl.BlockSpec(memory_space=pltpu.VMEM)
     return pl.pallas_call(
         kernel,
         out_shape=jax.ShapeDtypeStruct((HALF, RANK), F32),
-        in_specs=[smem_spec] * 4 + [pl.BlockSpec(memory_space=pl.ANY)] * 3,
+        in_specs=[pl.BlockSpec(memory_space=pl.ANY)] * 7,
         out_specs=vmem_spec,
         scratch_shapes=[
+            *[pltpu.SMEM((SLOTS,), jnp.int32)] * 4,
             vmem((SLOTS, BLOCK * MONTHS, BLOCK), jnp.bfloat16),
             vmem((2 * BLOCK, RANK), jnp.bfloat16),
             vmem((MONTHS, RANK), F32),
@@ -417,6 +431,7 @@
             vmem((4, HALF, RANK), F32),
             vmem((4, HALF, RANK), F32),
             vmem((3, HALF, RANK), F32),
+            dma((4,)),
             dma((SLOTS,)),
             dma((2,)),
             dma((2, 3)),

time: 52.1 us -> 49.7 us (0.954)
  Pallas kernels: 50.5 us -> 48.1 us
    pallas_call x1, Pallas kernels: 50.5 us -> 48.1 us  [local(): pl.pallas_call(kernel, out_shape=jax.ShapeDtypeStruct((HALF, RANK), F32),...]
where the time goes in v4:
time: 49.7 us; the launch traced here: 49.6 us
  Pallas kernels  48.1 us (97%)
  local copies, waits for them, and re-layouts  1.47 us (3%)
    pallas_call x1, Pallas kernels, local(): pl.pallas_call(kernel, out_shape=jax.ShapeDtypeStruct((HALF, RANK), F32),...  48.1 us
    unnamed x1, local copies, waits for them, and re-layouts  1.47 us

profile of v4, /device:TPU:1, one launch (start us, length us, event | category | flops | bytes accessed | tf_op | source)
XLA Modules:
  0.0 49.6 jit_solution(15319974368878449491)
XLA Ops:
  0.0 48.1 %shard_map.73 = f32[64,256]{1,0:T(8,128)} custom-call(s32[3]{0:T(128)} %bitcast.3, s32[3]{0:T(128)} %sub_in.1, s32[3]{0:T(128)} %block_in.1, s32[3]{0:T(128)} %live_in.1, bf16[3,15360,128]{2,1,0:T(8,128)(2,1)} %bitcast.2, bf16[256,256]{1,0:T(8,128)(2,1)} %code_in.1, f32[120,256]{1,0:T(8,128)} %month_in.1), custom_call_target="tpu_custom_call" | custom-call | flops 3300000000 | bytes 12000000 | tf_op jit(solution)/shard_map/pallas_call | solution.py:406
  48.1 1.5 %copy.9 = f32[64,256]{1,0:T(8,128)} copy(f32[64,256]{1,0:T(8,128)} %shard_map.73) | data formatting | bytes 131072

commit v5 on v4

--- a/solution.py
+++ b/solution.py
@@ -71,8 +71,7 @@
     return d
 
 
-def panel(rows, half, l0, row, lane):
-    c = [lane_of(rows[half], l0 + m) for m in range(8)]
+def panel(rows, half, l0, row, lane, c):
     lines = [[row_of(rows[h], m) for m in range(8)] for h in range(2)]
     d = sweep_pairs({(i, j): row_of(c[j], i) for i in range(8) for j in range(i, 8)})
     row_bits = [(row & b) == b for b in (1, 2, 4)]
@@ -84,7 +83,7 @@
     for h in range(2):
         w = -add_up([minus[m] * lines[h][m] for m in range(8)])
         out.append(jnp.where((rel >= 0) & (rel < 8), inside, w) if h == half else w)
-    return out
+    return out, minus
 
 
 def turned_dot(a, b):
@@ -121,7 +120,19 @@
             factor = {i: [lane_of(rows[i][0], l0 + m) for m in range(8)] for i in order}
             if beside is not None and j == 1:
                 beside(s)
-            rows[j] = panel(rows[j], 0, l0, row, lane)
+            ahead_of_rows = beside is None and j + 1 < n
+            if j == 0 or beside is not None:
+                block = [lane_of(rows[j][0], l0 + m) for m in range(8)]
+            if ahead_of_rows:
+                later = [lane_of(rows[j + 1][0], l0 + 8 + m) for m in range(8)]
+            rows[j], minus = panel(rows[j], 0, l0, row, lane, block)
+            if ahead_of_rows:
+                f = factor[j + 1]
+                scaled = [add_up([minus[p] * row_of(f[p], m) for p in range(8)]) for m in range(8)]
+                block = [
+                    later[m] + add_up([f[q] * row_of(scaled[m], q) for q in range(8)])
+                    for m in range(8)
+                ]
             inside = (lane >= l0) & (lane < l0 + 8)
             w = [[row_of(rows[j][h], m) for m in range(8)] for h in range(2)]
             for i in order:
@@ -200,9 +211,6 @@
             pltpu.make_async_copy(month_in, month, small_sem.at[1]),
         ]
     )
-    loads = start(
-        [pltpu.make_async_copy(tiles.at[k], counts.at[k], tile_sem.at[k]) for k in range(SLOTS)]
-    )
     scalars = start(
         [
             pltpu.make_async_copy(src, dst, scalar_sem.at[n])
@@ -219,6 +227,9 @@
         )
     for e in PLANE:
         pl.semaphore_signal(barrier, inc=1, device_id=plane(e)[0], device_id_type=MESH)
+    loads = start(
+        [pltpu.make_async_copy(tiles.at[k], counts.at[k], tile_sem.at[k]) for k in range(SLOTS)]
+    )
     for c in scalars:
         c.wait()
     line_at = lax.broadcasted_iota(jnp.int32, (8, 128), 0)
@@ -239,6 +250,10 @@
     for h in range(2):
         for b in range(2):
             group[h, mine[h] + b] = code[b * BLOCK : (b + 1) * BLOCK, h * BLOCK : (h + 1) * BLOCK]
+    own = lax.dot_general(
+        code[...], code[...], (((0,), (0,)), ((), ())), preferred_element_type=F32
+    )
+    gram_own[...] = own.reshape(32, 8, RANK)
     pl.semaphore_wait(barrier, 38)
 
     across = []
@@ -255,10 +270,6 @@
         ]
     )
 
-    own = lax.dot_general(
-        code[...], code[...], (((0,), (0,)), ((), ())), preferred_element_type=F32
-    )
-    gram_own[...] = own.reshape(32, 8, RANK)
 
     for e in PLANE:
         to, q = plane(e)
@@ -391,11 +402,18 @@
     carry = eliminate(gram, 0, 2 * per_half, carry, contract, send_sums)
     line = [line_copy(n, d) for n in range(per_half) for d in range(1, 4)]
     _, before, after = eliminate(gram, 2 * per_half, RANK // SIDE, carry)
-    clear_and_subtract(gram, RANK // SIDE - 1, before, after)
     for c in line:
         c.wait()
     share = line_out[zl] + line_in[0] + line_in[1] + line_in[2]
-    out[...] = -jnp.dot(share, gram[...], precision=HI, preferred_element_type=F32)
+    kept = lax.broadcasted_iota(jnp.int32, (1, RANK), 1) < RANK - SIDE
+    rest = jnp.where(kept, share, 0.0)
+    main = jnp.dot(
+        rest, jnp.where(kept, gram[...], 0.0), precision=HI, preferred_element_type=F32
+    )
+    last = share[:, RANK - SIDE :] - lax.dot_general(
+        rest, before, (((1,), (1,)), ((), ())), precision=HI, preferred_element_type=F32
+    )
+    out[...] = -(main + jnp.dot(last, after, precision=HI, preferred_element_type=F32))
     arrived(gram_own.at[0:31], plane_s)
     arrived(gram_own.at[0:15], spread_s)
 

time: 49.7 us -> 49.1 us (0.988)
  Pallas kernels: 48.1 us -> 47.5 us
    pallas_call x1, Pallas kernels: 48.1 us -> 47.5 us  [local(): pl.pallas_call(kernel, out_shape=jax.ShapeDtypeStruct((HALF, RANK), F32),...]
where the time goes in v5:
time: 49.1 us; the launch traced here: 49 us
  Pallas kernels  47.5 us (97%)
  local copies, waits for them, and re-layouts  1.47 us (3%)
    pallas_call x1, Pallas kernels, local(): pl.pallas_call(kernel, out_shape=jax.ShapeDtypeStruct((HALF, RANK), F32),...  47.5 us
    unnamed x1, local copies, waits for them, and re-layouts  1.47 us

profile of v5, /device:TPU:1, one launch (start us, length us, event | category | flops | bytes accessed | tf_op | source)
XLA Modules:
  0.0 49.0 jit_solution(2875268137563698670)
XLA Ops:
  0.0 47.5 %shard_map.73 = f32[64,256]{1,0:T(8,128)} custom-call(s32[3]{0:T(128)} %bitcast.3, s32[3]{0:T(128)} %sub_in.1, s32[3]{0:T(128)} %block_in.1, s32[3]{0:T(128)} %live_in.1, bf16[3,15360,128]{2,1,0:T(8,128)(2,1)} %bitcast.2, bf16[256,256]{1,0:T(8,128)(2,1)} %code_in.1, f32[120,256]{1,0:T(8,128)} %month_in.1), custom_call_target="tpu_custom_call" | custom-call | flops 3300000000 | bytes 12000000 | tf_op jit(solution)/shard_map/pallas_call | solution.py:424
  47.5 1.5 %copy.9 = f32[64,256]{1,0:T(8,128)} copy(f32[64,256]{1,0:T(8,128)} %shard_map.73) | data formatting | bytes 131072
